TPU v7x, 32 devices: a whole 2x2x4 slice. The times are simulated.
32 devices in a mesh: grp: 8 (over y, x, core), sl: 4 (over z).
Axes of the slice: x: 2, y: 2, z: 4, core: 2. Of those that a mesh axis runs over, the one named last changes fastest.
Arguments:
- tokens: bfloat16 [256, 3072], P('grp', 'sl'), may hold values from -6 to 6
- grad_out: bfloat16 [256, 3072], P('grp', 'sl'), may hold values from -6 to 6
- expert_ids: int32 [256, 2], P('grp'), may hold values from 0 to 7, all different within a row; in each aligned block of 32 rows (0 to 31, 32 to 63, ...) at most 16 rows name the same one
- gate_probs: float32 [256, 2], P('grp'), may hold values from 0.2 to 1
- gate_weight: bfloat16 [8, 18432, 3072], P('grp', 'sl'), may hold values from -0.109375 to 0.109375
- up_weight: bfloat16 [8, 18432, 3072], P('grp', 'sl'), may hold values from -0.109375 to 0.109375
- down_weight: bfloat16 [8, 18432, 3072], P('grp', 'sl'), may hold values from -0.046875 to 0.046875
Outputs:
- grad_input: bfloat16 [256, 3072], P('grp', 'sl')
- grad_down: bfloat16 [8, 18432, 3072], P('grp', 'sl')
Inputs may be any that keep to these rules, and one draw needn't show every extreme that they name: `expert_ids`: each token names two different experts. Among the 32 tokens of one group no expert is named more than 16 times, a bound that some block reaches.
All inputs are finite; a program needn't handle non-finite values.
Results may differ from a plain program's by a relative error of at most 0.0057.
Values may be sent and summed in bfloat16 or wider, within the bound.
A program may use at most 256 MiB of HBM per device.

v0:
```python
import jax
import jax.numpy as jnp
from jax import lax
from jax.sharding import PartitionSpec as P

EXPERTS = 8


def slot_numbers(group_ids):
    flat_ids = group_ids.reshape(-1)
    expert_list = jnp.arange(EXPERTS, dtype=jnp.int32)
    onehot = (flat_ids[:, None] == expert_list[None, :]).astype(jnp.int32)
    earlier = jnp.cumsum(onehot, axis=0) - onehot
    slot_of = jnp.sum(earlier * onehot, axis=1)
    return (flat_ids, slot_of)


def slot_table(flat_ids, slot_of, capacity):
    expert_list = jnp.arange(EXPERTS, dtype=jnp.int32)
    expert_hit = flat_ids[None, None, :] == expert_list[:, None, None]
    slot_hit = slot_of[None, None, :] == jnp.arange(capacity, dtype=jnp.int32)[None, :, None]
    return jnp.logical_and(expert_hit, slot_hit).astype(jnp.bfloat16)


def project(left, right):
    return lax.dot_general(
        left, right, (((1,), (1,)), ((), ())), preferred_element_type=jnp.float32
    )


def row_product(left, right):
    return lax.dot_general(
        left, right, (((0,), (0,)), ((), ())), preferred_element_type=jnp.float32
    )


def activations(gate_acts, up_acts):
    sigmoid_g = jax.nn.sigmoid(gate_acts)
    silu_g = gate_acts * sigmoid_g
    hidden = (silu_g * up_acts).astype(jnp.bfloat16)
    return (sigmoid_g, silu_g, hidden)


def local(tokens, grad_out, expert_ids, gate_probs, gate_weight, up_weight, down_weight):
    group_tokens, feature_cols = tokens.shape
    capacity = group_tokens // 2
    owners = lax.axis_size("grp") // EXPERTS
    flat_ids, slot_of = slot_numbers(expert_ids)
    selector = slot_table(flat_ids, slot_of, capacity)
    token_rows = jnp.repeat(tokens, 2, axis=0)
    scaled = (
        gate_probs.reshape(-1, 1) * jnp.repeat(grad_out, 2, axis=0).astype(jnp.float32)
    ).astype(jnp.bfloat16)
    packed_in = jnp.einsum(
        "eca,ad->ecd", selector, token_rows, preferred_element_type=jnp.float32
    ).astype(jnp.bfloat16)
    packed_grad = jnp.einsum(
        "eca,ad->ecd", selector, scaled, preferred_element_type=jnp.float32
    ).astype(jnp.bfloat16)
    send_in = jnp.repeat(packed_in, owners, axis=0)
    send_grad = jnp.repeat(packed_grad, owners, axis=0)
    recv_in, recv_grad = (
        lax.all_to_all(send_in, "grp", split_axis=0, concat_axis=0, tiled=True),
        lax.all_to_all(send_grad, "grp", split_axis=0, concat_axis=0, tiled=True),
    )
    row_count = recv_in.shape[0] * capacity
    rows_in = recv_in.reshape(row_count, feature_cols)
    rows_grad = recv_grad.reshape(row_count, feature_cols)
    gate_local = gate_weight[0]
    up_local = up_weight[0]
    down_local = down_weight[0]
    block_in = lax.all_gather(rows_in, "sl", axis=1, tiled=True)
    gate_acts = project(block_in, gate_local)
    up_acts = project(block_in, up_local)
    gate_acts, up_acts = (gate_acts, up_acts)
    sigmoid_g, silu_g, hidden = activations(gate_acts, up_acts)
    block_grad = lax.all_gather(rows_grad, "sl", axis=1, tiled=True)
    grad_hidden = project(block_grad, down_local)
    columns = row_product(hidden, block_grad)
    grad_hidden, grad_down = (grad_hidden, columns)
    grad_gate = (grad_hidden * up_acts * sigmoid_g * (1.0 + gate_acts * (1.0 - sigmoid_g))).astype(
        jnp.bfloat16
    )
    grad_up = (grad_hidden * silu_g).astype(jnp.bfloat16)
    shares = lax.psum_scatter(
        row_product(gate_local, jnp.transpose(grad_gate))
        + row_product(up_local, jnp.transpose(grad_up)),
        "sl",
        scatter_dimension=0,
        tiled=True,
    )
    outgoing = jnp.transpose(shares).reshape(-1, capacity, feature_cols)
    returned = lax.all_to_all(outgoing, "grp", split_axis=0, concat_axis=0, tiled=True)
    summed = returned.reshape(EXPERTS, owners, capacity, feature_cols).sum(axis=1)
    per_assign = summed[flat_ids, slot_of]
    grad_input = per_assign.reshape(group_tokens, 2, feature_cols).sum(axis=1).astype(jnp.bfloat16)
    return (grad_input, grad_down.astype(jnp.bfloat16)[None])


def solution(mesh):
    return jax.shard_map(
        local,
        mesh=mesh,
        in_specs=(
            P("grp", "sl"),
            P("grp", "sl"),
            P("grp", None),
            P("grp", None),
            P("grp", "sl", None),
            P("grp", "sl", None),
            P("grp", "sl", None),
        ),
        out_specs=(P("grp", "sl"), P("grp", "sl", None)),
        check_vma=False,
    )
```

profile of v0, /device:TPU:0, one launch (start us, length us, event | category | flops | bytes accessed | tf_op | source)
XLA Modules:
  0.0 203.3 jit_solution(1130533340032700474)
XLA Ops:
  7.2 0.8 copy.12
  8.1 0.8 copy.13
  9.1 0.2 select_reduce_fusion
  9.3 0.5 copy-done.2
  9.8 0.9 broadcast_in_dim.6
  10.6 0.1 convert_element_type.37
  10.8 0.9 convolution_convert_fusion.2
  11.7 5.2 %all-to-all-start = ((bf16[8,16,768]{2,1,0:T(8,128)(2,1)}), bf16[8,16,768]{2,1,0:T(8,128)(2,1)S(1)}, u32[]{:S(2)}, u32[]{:S(2)}) async-start(bf16[8,16,768]{2,1,0:T(8,128)(2,1)} %convolution_convert_fusion.2), calls=%async_computation | async-start | bytes 393216 | tf_op jit(solution)/shard_map/all_to_all | solution.py:64
  16.9 0.9 broadcast_in_dim.7
  17.8 0.9 convolution_convert_fusion.1
  18.6 4.5 %all-to-all-done = bf16[8,16,768]{2,1,0:T(8,128)(2,1)S(1)} async-done(((bf16[8,16,768]{2,1,0:T(8,128)(2,1)}), bf16[8,16,768]{2,1,0:T(8,128)(2,1)S(1)}, u32[]{:S(2)}, u32[]{:S(2)}) %all-to-all-start) | async-done | bytes 196640 | tf_op jit(solution)/shard_map/all_to_all | solution.py:64
  23.1 3.4 %all-to-all-start.1 = ((bf16[8,16,768]{2,1,0:T(8,128)(2,1)}), bf16[8,16,768]{2,1,0:T(8,128)(2,1)S(1)}, u32[]{:S(2)}, u32[]{:S(2)}) async-start(bf16[8,16,768]{2,1,0:T(8,128)(2,1)} %convolution_convert_fusion.1), calls=%async_computation.1 | async-start | bytes 393216 | tf_op jit(solution)/shard_map/all_to_all | solution.py:63
  26.6 20.2 %all_gather.6 = bf16[128,3072]{1,0:T(8,128)(2,1)} all-gather(bf16[128,768]{1,0:T(8,128)(2,1)S(1)} %bitcast.40), channel_id=1, replica_groups=mesh['grp'=8,'sl'=4] {'sl'}, dimensions={1}, use_global_device_ids=true | all-gather | bytes 983040 | tf_op jit(solution)/shard_map/all_gather | solution.py:77
  46.8 18.4 %all_gather.7 = bf16[128,3072]{1,0:T(8,128)(2,1)S(1)} all-gather(bf16[128,768]{1,0:T(8,128)(2,1)S(1)} %bitcast.41), channel_id=1, replica_groups=mesh['grp'=8,'sl'=4] {'sl'}, dimensions={1}, use_global_device_ids=true | all-gather | bytes 983040 | tf_op jit(solution)/shard_map/all_gather | solution.py:72
  65.2 14.6 %fusion.2 = f32[128,4608]{1,0:T(8,128)S(1)} fusion(bf16[128,3072]{1,0:T(8,128)(2,1)S(1)} %all_gather.7, bf16[1,4608,3072]{2,1,0:T(8,128)(2,1)} %param.11), kind=kOutput, calls=%fused_computation.4 | convolution fusion | flops 3623878656 | bytes 31457280 | tf_op jit(solution)/shard_map/dot_general | solution.py:26
  79.9 16.0 %fusion.6 = f32[128,4608]{1,0:T(8,128)} fusion(bf16[128,3072]{1,0:T(8,128)(2,1)S(1)} %all_gather.7, bf16[1,4608,3072]{2,1,0:T(8,128)(2,1)} %param.12), kind=kOutput, calls=%fused_computation.8 | convolution fusion | flops 3623878656 | bytes 31457280 | tf_op jit(solution)/shard_map/dot_general | solution.py:26
  95.9 15.8 %fusion.8 = f32[128,4608]{1,0:T(8,128)} fusion(bf16[128,3072]{1,0:T(8,128)(2,1)} %all_gather.6, bf16[1,4608,3072]{2,1,0:T(8,128)(2,1)} %param.13), kind=kOutput, calls=%fused_computation.10 | convolution fusion | flops 3623878656 | bytes 31457280 | tf_op jit(solution)/shard_map/dot_general | solution.py:26
  111.7 15.2 %fusion = f32[128,3072]{1,0:T(8,128)S(1)} fusion(bf16[1,4608,3072]{2,1,0:T(8,128)(2,1)} %param.11, f32[128,4608]{1,0:T(8,128)S(1)} %fusion.2, f32[128,4608]{1,0:T(8,128)} %fusion.8, f32[128,4608]{1,0:T(8,128)} %fusion.6), kind=kOutput, calls=%fused_computation.2 | convolution fusion | flops 3629776896 | bytes 36962304 | tf_op jit(solution)/shard_map/dot_general | solution.py:32
  126.8 14.4 %fusion.14 = f32[3072,128]{0,1:T(8,128)} fusion(f32[128,3072]{1,0:T(8,128)S(1)} %fusion, bf16[1,4608,3072]{2,1,0:T(8,128)(2,1)} %param.12, f32[128,4608]{1,0:T(8,128)S(1)} %copy-done.1, f32[128,4608]{1,0:T(8,128)S(1)} %fusion.2), kind=kOutput, calls=%fused_computation.14 | convolution fusion | flops 3627810816 | bytes 36175872 | tf_op jit(solution)/shard_map/dot_general | solution.py:32
  141.4 34.9 %reduce-scatter.2.cloned.1.call-done = f32[768,128]{0,1:T(8,128)} async-done(((f32[3072,128]{0,1:T(8,128)}), f32[768,128]{0,1:T(8,128)}) %reduce-scatter.2.cloned.1.call-update) | async-done | bytes 393232 | tf_op jit(solution)/shard_map/reduce_scatter | solution.py:85
  176.3 3.7 %all-to-all-start.2 = ((f32[8,16,768]{2,1,0:T(8,128)}), f32[8,16,768]{2,1,0:T(8,128)S(1)}, u32[]{:S(2)}, u32[]{:S(2)}) async-start(f32[8,16,768]{2,1,0:T(8,128)} %bitcast.42), calls=%async_computation.3 | async-start | bytes 786432 | tf_op jit(solution)/shard_map/all_to_all | solution.py:93
  180.0 14.5 %fusion.10 = bf16[1,4608,3072]{2,1,0:T(8,128)(2,1)} fusion(bf16[128,3072]{1,0:T(8,128)(2,1)S(1)} %copy-done, f32[128,4608]{1,0:T(8,128)} %fusion.6, f32[128,4608]{1,0:T(8,128)S(1)} %fusion.2), kind=kOutput, calls=%fused_computation.12 | convolution fusion | flops 3641573376 | bytes 33816576 | tf_op jit(solution)/shard_map/dot_general | solution.py:32
  194.5 1.0 gather_fusion
  195.6 0.9 reduce_sum.26
  (21 shorter events, 0.7 us)
Async XLA Ops:
  9.3 0.5 copy-start.2
  11.7 11.4 %all-to-all-start = ((bf16[8,16,768]{2,1,0:T(8,128)(2,1)}), bf16[8,16,768]{2,1,0:T(8,128)(2,1)S(1)}, u32[]{:S(2)}, u32[]{:S(2)}) async-start(bf16[8,16,768]{2,1,0:T(8,128)(2,1)} %convolution_convert_fusion.2), calls=%async_computation | async-start | bytes 393216 | tf_op jit(solution)/shard_map/all_to_all | solution.py:64
  23.1 23.7 %all-to-all-start.1 = ((bf16[8,16,768]{2,1,0:T(8,128)(2,1)}), bf16[8,16,768]{2,1,0:T(8,128)(2,1)S(1)}, u32[]{:S(2)}, u32[]{:S(2)}) async-start(bf16[8,16,768]{2,1,0:T(8,128)(2,1)} %convolution_convert_fusion.1), calls=%async_computation.1 | async-start | bytes 393216 | tf_op jit(solution)/shard_map/all_to_all | solution.py:63
  26.5 149.8 %reduce-scatter.2.cloned.1.call-start = ((), (), s32[]{:S(2)}) async-start(), calls=%async_computation.4 | async-start | bytes 1966080 | tf_op jit(solution)/shard_map/reduce_scatter | solution.py:85
  111.7 15.2 %copy-start.1 = (f32[128,4608]{1,0:T(8,128)S(1)}, f32[128,4608]{1,0:T(8,128)}, u32[]{:S(2)}) copy-start(f32[128,4608]{1,0:T(8,128)} %fusion.8) | copy-start | bytes 7077892
  126.8 14.5 %copy-start.3 = (s32[64]{0:T(128)S(1)}, s32[64]{0:T(128)}, u32[]{:S(2)}) copy-start(s32[64]{0:T(128)} %copy-done.2) | copy-start | bytes 772
  141.2 38.7 %copy-start = (bf16[128,3072]{1,0:T(8,128)(2,1)S(1)}, bf16[128,3072]{1,0:T(8,128)(2,1)}, u32[]{:S(2)}) copy-start(bf16[128,3072]{1,0:T(8,128)(2,1)} %all_gather.6) | copy-start | bytes 2359300
  176.3 18.2 %all-to-all-start.2 = ((f32[8,16,768]{2,1,0:T(8,128)}), f32[8,16,768]{2,1,0:T(8,128)S(1)}, u32[]{:S(2)}, u32[]{:S(2)}) async-start(f32[8,16,768]{2,1,0:T(8,128)} %bitcast.42), calls=%async_computation.3 | async-start | bytes 786432 | tf_op jit(solution)/shard_map/all_to_all | solution.py:93
Sparse Core Ops, SparseCore 0:
  141.4 34.8 reduce-scatter.1
where the time goes:
time: 204 us; the launch traced here: 203 us
  matrix products  92.3 us (45%)
  waiting for transfers between devices  39.4 us (19%)
  blocking collectives  38.6 us (19%)
  between operations  14.2 us (7%)
  starting transfers between devices  12.3 us (6%)
  local copies, waits for them, and re-layouts  5.31 us (3%)
    dot_general x3, matrix products, project(): lax.dot_general(left, right, (((1,), (1,)), ((), ())), preferred_element_...  46.4 us
    dot_general x3, matrix products, row_product(): lax.dot_general(left, right, (((0,), (0,)), ((), ())), preferred_element_...  44.1 us
    reduce_scatter x1, waiting for transfers between devices, local(): lax.psum_scatter(row_product(gate_local, jnp.transpose(grad_gate)) + row_...  34.9 us
    all_gather x1, blocking collectives, local(): block_grad = lax.all_gather(rows_grad, 'sl', axis=1, tiled=True)  20.2 us
    all_gather x1, blocking collectives, local(): block_in = lax.all_gather(rows_in, 'sl', axis=1, tiled=True)  18.4 us
    all_to_all x1, starting transfers between devices, local(): lax.all_to_all(send_grad, 'grp', split_axis=0, concat_axis=0, tiled=True)  5.17 us
    all_to_all x1, waiting for transfers between devices, local(): lax.all_to_all(send_grad, 'grp', split_axis=0, concat_axis=0, tiled=True)  4.46 us
  transfers between devices with their start and end apart: 4, of which 2 were waited for; matrix products, arithmetic and copies ran while one was open for 8% of the time, Pallas kernels for 0%

commit v1 on v0

v1 whole, which is shorter than its diff:
```python
import functools

import jax
import jax.numpy as jnp
from jax import lax
from jax.experimental import pallas as pl
from jax.experimental.pallas import tpu as pltpu
from jax.sharding import PartitionSpec as P

EXPERTS = 8
MESH = pl.DeviceIdType.MESH
BIG = 56 * 1024 * 1024


def greet(n_g, n_s):
    g, s = lax.axis_index("grp"), lax.axis_index("sl")
    barrier = pltpu.get_barrier_semaphore()

    @pl.loop(1, n_g)
    def _(j):
        pl.semaphore_signal(
            barrier, inc=1, device_id=(lax.rem(g + j, n_g), s), device_id_type=MESH
        )

    @pl.loop(1, n_s)
    def _(j):
        pl.semaphore_signal(
            barrier, inc=1, device_id=(g, lax.rem(s + j, n_s)), device_id_type=MESH
        )

    pl.semaphore_wait(barrier, n_g - 1 + n_s - 1)


def slots(ids_ref):
    count = ids_ref.shape[0]
    first, second = ids_ref[:, 0:1], ids_ref[:, 1:2]
    lane = lax.broadcasted_iota(jnp.int32, (count, 128), 1)
    hit0 = (lane == first).astype(jnp.float32)
    hit1 = (lane == second).astype(jnp.float32)
    row = lax.broadcasted_iota(jnp.int32, (count, count), 0)
    col = lax.broadcasted_iota(jnp.int32, (count, count), 1)
    before = (col < row).astype(jnp.float32)
    earlier = jnp.dot(before, hit0 + hit1, preferred_element_type=jnp.float32)
    slot0 = jnp.sum(earlier * hit0, axis=1, keepdims=True).astype(jnp.int32)
    slot1 = jnp.sum(earlier * hit1, axis=1, keepdims=True).astype(jnp.int32)
    return first, second, slot0, slot1


def pick(expert, slot, cap, owners, width):
    lane = lax.broadcasted_iota(jnp.int32, (expert.shape[0], width), 1)
    table = jnp.zeros((expert.shape[0], width), jnp.float32)
    for owner in range(owners):
        table = table + (lane == (expert * owners + owner) * cap + slot).astype(jnp.float32)
    return table.astype(jnp.bfloat16)


def over_rows(left, right):
    return lax.dot_general(
        left, right, (((0,), (0,)), ((), ())), preferred_element_type=jnp.float32
    )


def dispatch_kernel(
    n_g, n_s, tok_ref, grad_ref, ids_ref, prob_ref, out_ref,
    raw, stage, table, send_a, recv_a, send_b, recv_b,
):
    g, s = lax.axis_index("grp"), lax.axis_index("sl")
    count, fc = tok_ref.shape
    cap = count // 2
    owners = n_g // EXPERTS
    greet(n_g, n_s)

    @pl.loop(1, n_s)
    def _(k):
        peer = lax.rem(s + k, n_s)
        for part, ref in enumerate((tok_ref, grad_ref)):
            pltpu.make_async_remote_copy(
                src_ref=ref, dst_ref=raw.at[s, part], send_sem=send_a, recv_sem=recv_a.at[s],
                device_id=(g, peer), device_id_type=MESH,
            ).start()

    first, second, slot0, slot1 = slots(ids_ref)
    table[0] = pick(first, slot0, cap, 1, EXPERTS * cap)
    table[1] = pick(second, slot1, cap, 1, EXPERTS * cap)

    def pack(src, tokens, grads):
        sel0, sel1 = table[0], table[1]
        wide = grads.astype(jnp.float32)
        scaled0 = (prob_ref[:, 0:1] * wide).astype(jnp.bfloat16)
        scaled1 = (prob_ref[:, 1:2] * wide).astype(jnp.bfloat16)
        stage[src, 0] = over_rows(sel0 + sel1, tokens).astype(jnp.bfloat16)
        stage[src, 1] = (over_rows(sel0, scaled0) + over_rows(sel1, scaled1)).astype(jnp.bfloat16)
        columns = pl.ds(pl.multiple_of(src * fc, 128), fc)
        mine = pl.ds(pl.multiple_of(g * cap, 16), cap)

        @pl.loop(1, n_g)
        def _(j):
            dest = lax.rem(g + j, n_g)
            theirs = pl.ds(pl.multiple_of((dest // owners) * cap, 16), cap)
            pltpu.make_async_remote_copy(
                src_ref=stage.at[src, :, theirs, :],
                dst_ref=out_ref.at[:, mine, columns],
                send_sem=send_b, recv_sem=recv_b,
                device_id=(dest, s), device_id_type=MESH,
            ).start()

        own = pl.ds(pl.multiple_of((g // owners) * cap, 16), cap)
        out_ref[0, mine, columns] = stage[src, 0, own, :]
        out_ref[1, mine, columns] = stage[src, 1, own, :]

    pack(s, tok_ref[...], grad_ref[...])

    @pl.loop(1, n_s)
    def _(k):
        src = lax.rem(s + k, n_s)
        pltpu.make_async_copy(raw.at[src], raw.at[src], recv_a.at[src]).wait()
        pack(src, raw[src, 0], raw[src, 1])

    sent = raw.at[pl.ds(0, n_s - 1)]
    pltpu.make_async_copy(sent, sent, send_a).wait()
    rest = out_ref.at[:, pl.ds(0, (n_g - 1) * cap), :]
    pltpu.make_async_copy(rest, rest, send_b).wait()
    pltpu.make_async_copy(rest, rest, recv_b).wait()


def expert_kernel(xg_ref, gate_ref, up_ref, down_ref, grad_down_ref, part_ref, total):
    step = pl.program_id(0)
    rows_in, rows_grad = xg_ref[0], xg_ref[1]
    over_features = (((1,), (1,)), ((), ()))
    gate_w, up_w, down_w = gate_ref[0], up_ref[0], down_ref[0]
    gate = lax.dot_general(rows_in, gate_w, over_features, preferred_element_type=jnp.float32)
    up = lax.dot_general(rows_in, up_w, over_features, preferred_element_type=jnp.float32)
    dhid = lax.dot_general(rows_grad, down_w, over_features, preferred_element_type=jnp.float32)
    sig = jax.nn.sigmoid(gate)
    silu = gate * sig
    hidden = (silu * up).astype(jnp.bfloat16)
    dgate = (dhid * up * sig * (1.0 + gate * (1.0 - sig))).astype(jnp.bfloat16)
    dup = (dhid * silu).astype(jnp.bfloat16)
    grad_down_ref[0] = over_rows(hidden, rows_grad).astype(jnp.bfloat16)
    term = jnp.dot(dgate, gate_w, preferred_element_type=jnp.float32) + jnp.dot(
        dup, up_w, preferred_element_type=jnp.float32
    )

    @pl.when(step == 0)
    def _():
        total[...] = term

    @pl.when(step > 0)
    def _():
        total[...] += term

    @pl.when(step == pl.num_programs(0) - 1)
    def _():
        part_ref[...] = total[...].astype(jnp.bfloat16)


def return_kernel(
    n_g, n_s, part_ref, ids_ref, out_ref, back, table, shares, got, send_a, recv_a, send_b, recv_b
):
    g, s = lax.axis_index("grp"), lax.axis_index("sl")
    count, fc = out_ref.shape
    cap = count // 2
    owners = n_g // EXPERTS
    greet(n_g, n_s)
    mine = pl.ds(pl.multiple_of(g * cap, 16), cap)

    @pl.loop(1, n_s + 1)
    def _(k):
        chunk = lax.rem(s + k, n_s)
        columns = pl.ds(pl.multiple_of(chunk * fc, 128), fc)

        @pl.loop(1, n_g)
        def _(j):
            dest = lax.rem(g + j, n_g)
            theirs = pl.ds(pl.multiple_of(dest * cap, 16), cap)
            pltpu.make_async_remote_copy(
                src_ref=part_ref.at[theirs, columns],
                dst_ref=back.at[chunk, mine, :],
                send_sem=send_a, recv_sem=recv_a.at[chunk],
                device_id=(dest, s), device_id_type=MESH,
            ).start()

        back[chunk, mine, :] = part_ref[mine, columns]

    first, second, slot0, slot1 = slots(ids_ref)
    width = n_g * cap
    table[...] = pick(first, slot0, cap, owners, width) + pick(second, slot1, cap, owners, width)

    def arrived(chunk):
        whole = back.at[chunk, pl.ds(0, (n_g - 1) * cap), :]
        pltpu.make_async_copy(whole, whole, recv_a.at[chunk]).wait()
        return jnp.dot(table[...], back[chunk], preferred_element_type=jnp.float32)

    @pl.loop(1, n_s)
    def _(k):
        chunk = lax.rem(s + k, n_s)
        shares[chunk] = arrived(chunk).astype(jnp.bfloat16)
        pltpu.make_async_remote_copy(
            src_ref=shares.at[chunk], dst_ref=got.at[s], send_sem=send_b, recv_sem=recv_b.at[s],
            device_id=(g, chunk), device_id_type=MESH,
        ).start()

    total = arrived(s)

    def add(k, total):
        src = lax.rem(s + k, n_s)
        pltpu.make_async_copy(got.at[src], got.at[src], recv_b.at[src]).wait()
        return total + got[src].astype(jnp.float32)

    total = lax.fori_loop(1, n_s, add, total)
    out_ref[...] = total.astype(jnp.bfloat16)
    sent = back.at[:, pl.ds(0, (n_g - 1) * cap), :]
    pltpu.make_async_copy(sent, sent, send_a).wait()
    shared = shares.at[pl.ds(0, n_s - 1)]
    pltpu.make_async_copy(shared, shared, send_b).wait()


def block_of(hidden):
    for size in (512, 384, 256, 192, 128):
        if hidden % size == 0:
            return size
    return hidden


def local(n_g, n_s, tokens, grad_out, expert_ids, gate_probs, gate_weight, up_weight, down_weight):
    count, fc = tokens.shape
    cap = count // 2
    rows = n_g * cap
    hidden, width = gate_weight.shape[1:]
    bf16 = jnp.bfloat16
    vmem = pl.BlockSpec(memory_space=pltpu.VMEM)
    dma = pltpu.SemaphoreType.DMA
    xg = pl.pallas_call(
        functools.partial(dispatch_kernel, n_g, n_s),
        out_shape=jax.ShapeDtypeStruct((2, rows, width), bf16),
        in_specs=[vmem] * 4,
        out_specs=vmem,
        scratch_shapes=[
            pltpu.VMEM((n_s, 2, count, fc), bf16),
            pltpu.VMEM((n_s, 2, EXPERTS * cap, fc), bf16),
            pltpu.VMEM((2, count, EXPERTS * cap), bf16),
            dma, dma((n_s,)), dma, dma,
        ],
        compiler_params=pltpu.CompilerParams(
            collective_id=0, has_side_effects=True, vmem_limit_bytes=BIG
        ),
        name="dispatch",
    )(tokens, grad_out, expert_ids, gate_probs)

    block = block_of(hidden)
    steps = hidden // block
    weight = pl.BlockSpec((1, block, width), lambda i: (0, i, 0))
    grad_down, part = pl.pallas_call(
        expert_kernel,
        grid=(steps,),
        out_shape=(
            jax.ShapeDtypeStruct((1, hidden, width), bf16),
            jax.ShapeDtypeStruct((rows, width), bf16),
        ),
        in_specs=[pl.BlockSpec((2, rows, width), lambda i: (0, 0, 0)), weight, weight, weight],
        out_specs=(weight, pl.BlockSpec((rows, width), lambda i: (0, 0))),
        scratch_shapes=[pltpu.VMEM((rows, width), jnp.float32)],
        compiler_params=pltpu.CompilerParams(
            dimension_semantics=("arbitrary",), vmem_limit_bytes=BIG
        ),
        name="experts",
    )(xg, gate_weight, up_weight, down_weight)

    grad_input = pl.pallas_call(
        functools.partial(return_kernel, n_g, n_s),
        out_shape=jax.ShapeDtypeStruct((count, fc), bf16),
        in_specs=[vmem] * 2,
        out_specs=vmem,
        scratch_shapes=[
            pltpu.VMEM((n_s, rows, fc), bf16),
            pltpu.VMEM((count, rows), bf16),
            pltpu.VMEM((n_s, count, fc), bf16),
            pltpu.VMEM((n_s, count, fc), bf16),
            dma, dma((n_s,)), dma, dma((n_s,)),
        ],
        compiler_params=pltpu.CompilerParams(
            collective_id=1, has_side_effects=True, vmem_limit_bytes=BIG
        ),
        name="give_back",
    )(part, expert_ids)
    return grad_input, grad_down


def solution(mesh):
    return jax.shard_map(
        functools.partial(local, mesh.shape["grp"], mesh.shape["sl"]),
        mesh=mesh,
        in_specs=(
            P("grp", "sl"),
            P("grp", "sl"),
            P("grp", None),
            P("grp", None),
            P("grp", "sl", None),
            P("grp", "sl", None),
            P("grp", "sl", None),
        ),
        out_specs=(P("grp", "sl"), P("grp", "sl", None)),
        check_vma=False,
    )
```

time: 204 us -> 105 us (0.51)
  Pallas kernels: 0 us -> 100 us
  matrix products: 92.3 us -> 0 us
  waiting for transfers between devices: 39.4 us -> 0 us
  blocking collectives: 38.6 us -> 0 us
  between operations: 14.2 us -> 0.65 us
  starting transfers between devices: 12.3 us -> 0 us
    pallas_call x0 -> x3, Pallas kernels: none -> 100 us  [the longest x1 53.5 us: local(): pl.pallas_call(expert_kernel, grid=(steps,), out_shape=(jax.ShapeDtypeStr...]
    dot_general x8 -> x0, matrix products: 92.3 us -> none  [the longest x3 46.4 us: project(): lax.dot_general(left, right, (((1,), (1,)), ((), ())), preferred_element_...]
    all_gather x2 -> x0, blocking collectives: 38.6 us -> none  [the longest x1 20.2 us: local(): block_grad = lax.all_gather(rows_grad, 'sl', axis=1, tiled=True)]
    reduce_scatter x1 -> x0, waiting for transfers between devices: 34.9 us -> none  [local(): lax.psum_scatter(row_product(gate_local, jnp.transpose(grad_gate)) + row_...]
    all_to_all x3 -> x0, starting transfers between devices: 12.2 us -> none  [the longest x1 5.17 us: local(): lax.all_to_all(send_grad, 'grp', split_axis=0, concat_axis=0, tiled=True)]
    all_to_all x3 -> x0, waiting for transfers between devices: 4.47 us -> none  [the longest x1 4.46 us: local(): lax.all_to_all(send_grad, 'grp', split_axis=0, concat_axis=0, tiled=True)]
    unnamed x10 -> x3, local copies, waits for them, and re-layouts: 2.04 us -> 4.15 us
  transfers between devices with their start and end apart: 4 -> 0, of which waited for: 2 -> 0; matrix products, arithmetic and copies ran while one was open for 8% -> 0% of each run, Pallas kernels for 0% -> 0%
where the time goes in v1:
time: 105 us
  Pallas kernels  100 us (95%)
  local copies, waits for them, and re-layouts  4.15 us (4%)
    pallas_call x1, Pallas kernels, local(): pl.pallas_call(expert_kernel, grid=(steps,), out_shape=(jax.ShapeDtypeStr...  53.5 us
    pallas_call x1, Pallas kernels, local(): pl.pallas_call(functools.partial(dispatch_kernel, n_g, n_s), out_shape=ja...  27.7 us
    pallas_call x1, Pallas kernels, local(): pl.pallas_call(functools.partial(return_kernel, n_g, n_s), out_shape=jax....  19.2 us
    unnamed x3, local copies, waits for them, and re-layouts  4.15 us

profile of v1, /device:TPU:0, one launch (start us, length us, event | category | flops | bytes accessed | tf_op | source)
XLA Modules:
  0.0 105.2 jit_solution(10967817454857121837)
XLA Ops:
  0.6 1.4 %copy.9.ids_ref = s32[32,2]{1,0:T(8,128)} copy(s32[32,2]{0,1:T(2,128)} %param.9) | data formatting | bytes 512 | tf_op args[2]
  2.0 1.4 %copy.10.prob_ref = f32[32,2]{1,0:T(8,128)} copy(f32[32,2]{0,1:T(2,128)} %param.10) | data formatting | bytes 512 | tf_op args[3]
  3.4 27.7 %dispatch.1.xg_ref = bf16[2,128,3072]{2,1,0:T(8,128)(2,1)} custom-call(bf16[32,768]{1,0:T(8,128)(2,1)} %tok_ref.1, bf16[32,768]{1,0:T(8,128)(2,1)} %grad_ref.1, s32[32,2]{1,0:T(8,128)} %copy.9.ids_ref, f32[32,2]{1,0:T(8,128)} %copy.10.prob_ref), custom_call_target="tpu_custom_call" | custom-call | tf_op jit(solution)/shard_map/dispatch/pallas_call | solution.py:233
  31.1 53.5 %experts.1 = (bf16[1,4608,3072]{2,1,0:T(8,128)(2,1)}, bf16[128,3072]{1,0:T(8,128)(2,1)}) custom-call(bf16[2,128,3072]{2,1,0:T(8,128)(2,1)} %dispatch.1.xg_ref, bf16[1,4608,3072]{2,1,0:T(8,128)(2,1)} %gate_ref.1, bf16[1,4608,3072]{2,1,0:T(8,128)(2,1)} %up_ref.1, bf16[1,4608,3072]{2,1,0:T(8,128)(2,1)} %down_ref.1), custom_call_target="tpu_custom_call" | custom-call | tf_op jit(solution)/shard_map/experts/pallas_call | solution.py:253
  84.6 19.2 %give_back.1 = bf16[32,768]{1,0:T(8,128)(2,1)} custom-call(bf16[128,3072]{1,0:T(8,128)(2,1)} %get-tuple-element.4.part_ref, s32[32,2]{1,0:T(8,128)} %copy.9.ids_ref), custom_call_target="tpu_custom_call" | custom-call | tf_op jit(solution)/shard_map/give_back/pallas_call | solution.py:269
  103.8 1.4 %copy.13 = bf16[32,768]{1,0:T(8,128)(2,1)} copy(bf16[32,768]{1,0:T(8,128)(2,1)} %give_back.1) | data formatting | bytes 98304

commit v2 on v1

--- a/solution.py
+++ b/solution.py
@@ -28,12 +28,21 @@
             barrier, inc=1, device_id=(g, lax.rem(s + j, n_s)), device_id_type=MESH
         )
 
-    pl.semaphore_wait(barrier, n_g - 1 + n_s - 1)
+
+def met(n_g, n_s):
+    pl.semaphore_wait(pltpu.get_barrier_semaphore(), n_g - 1 + n_s - 1)
+
+
+def upright(row):
+    count = row.shape[1]
+    here = lax.broadcasted_iota(jnp.int32, (count, count), 0)
+    there = lax.broadcasted_iota(jnp.int32, (count, count), 1)
+    return jnp.sum(jnp.where(here == there, row, jnp.zeros_like(row)), axis=1, keepdims=True)
 
 
 def slots(ids_ref):
-    count = ids_ref.shape[0]
-    first, second = ids_ref[:, 0:1], ids_ref[:, 1:2]
+    count = ids_ref.shape[1]
+    first, second = upright(ids_ref[0:1, :]), upright(ids_ref[1:2, :])
     lane = lax.broadcasted_iota(jnp.int32, (count, 128), 1)
     hit0 = (lane == first).astype(jnp.float32)
     hit1 = (lane == second).astype(jnp.float32)
@@ -69,29 +78,22 @@
     cap = count // 2
     owners = n_g // EXPERTS
     greet(n_g, n_s)
-
-    @pl.loop(1, n_s)
-    def _(k):
-        peer = lax.rem(s + k, n_s)
-        for part, ref in enumerate((tok_ref, grad_ref)):
-            pltpu.make_async_remote_copy(
-                src_ref=ref, dst_ref=raw.at[s, part], send_sem=send_a, recv_sem=recv_a.at[s],
-                device_id=(g, peer), device_id_type=MESH,
-            ).start()
-
     first, second, slot0, slot1 = slots(ids_ref)
     table[0] = pick(first, slot0, cap, 1, EXPERTS * cap)
     table[1] = pick(second, slot1, cap, 1, EXPERTS * cap)
+    prob0, prob1 = upright(prob_ref[0:1, :]), upright(prob_ref[1:2, :])
+    mine = pl.ds(pl.multiple_of(g * cap, 16), cap)
 
     def pack(src, tokens, grads):
         sel0, sel1 = table[0], table[1]
         wide = grads.astype(jnp.float32)
-        scaled0 = (prob_ref[:, 0:1] * wide).astype(jnp.bfloat16)
-        scaled1 = (prob_ref[:, 1:2] * wide).astype(jnp.bfloat16)
+        scaled0 = (prob0 * wide).astype(jnp.bfloat16)
+        scaled1 = (prob1 * wide).astype(jnp.bfloat16)
         stage[src, 0] = over_rows(sel0 + sel1, tokens).astype(jnp.bfloat16)
         stage[src, 1] = (over_rows(sel0, scaled0) + over_rows(sel1, scaled1)).astype(jnp.bfloat16)
+
+    def send(src):
         columns = pl.ds(pl.multiple_of(src * fc, 128), fc)
-        mine = pl.ds(pl.multiple_of(g * cap, 16), cap)
 
         @pl.loop(1, n_g)
         def _(j):
@@ -109,12 +111,25 @@
         out_ref[1, mine, columns] = stage[src, 1, own, :]
 
     pack(s, tok_ref[...], grad_ref[...])
+    met(n_g, n_s)
+
+    @pl.loop(1, n_s)
+    def _(k):
+        peer = lax.rem(s + k, n_s)
+        for part, ref in enumerate((tok_ref, grad_ref)):
+            pltpu.make_async_remote_copy(
+                src_ref=ref, dst_ref=raw.at[s, part], send_sem=send_a, recv_sem=recv_a.at[s],
+                device_id=(g, peer), device_id_type=MESH,
+            ).start()
+
+    send(s)
 
     @pl.loop(1, n_s)
     def _(k):
         src = lax.rem(s + k, n_s)
         pltpu.make_async_copy(raw.at[src], raw.at[src], recv_a.at[src]).wait()
         pack(src, raw[src, 0], raw[src, 1])
+        send(src)
 
     sent = raw.at[pl.ds(0, n_s - 1)]
     pltpu.make_async_copy(sent, sent, send_a).wait()
@@ -128,17 +143,19 @@
     rows_in, rows_grad = xg_ref[0], xg_ref[1]
     over_features = (((1,), (1,)), ((), ()))
     gate_w, up_w, down_w = gate_ref[0], up_ref[0], down_ref[0]
-    gate = lax.dot_general(rows_in, gate_w, over_features, preferred_element_type=jnp.float32)
-    up = lax.dot_general(rows_in, up_w, over_features, preferred_element_type=jnp.float32)
-    dhid = lax.dot_general(rows_grad, down_w, over_features, preferred_element_type=jnp.float32)
+    gate = lax.dot_general(gate_w, rows_in, over_features, preferred_element_type=jnp.float32)
+    up = lax.dot_general(up_w, rows_in, over_features, preferred_element_type=jnp.float32)
+    dhid = lax.dot_general(down_w, rows_grad, over_features, preferred_element_type=jnp.float32)
     sig = jax.nn.sigmoid(gate)
     silu = gate * sig
     hidden = (silu * up).astype(jnp.bfloat16)
     dgate = (dhid * up * sig * (1.0 + gate * (1.0 - sig))).astype(jnp.bfloat16)
     dup = (dhid * silu).astype(jnp.bfloat16)
-    grad_down_ref[0] = over_rows(hidden, rows_grad).astype(jnp.bfloat16)
-    term = jnp.dot(dgate, gate_w, preferred_element_type=jnp.float32) + jnp.dot(
-        dup, up_w, preferred_element_type=jnp.float32
+    grad_down_ref[0] = jnp.dot(hidden, rows_grad, preferred_element_type=jnp.float32).astype(
+        jnp.bfloat16
+    )
+    term = jnp.dot(dgate.T, gate_w, preferred_element_type=jnp.float32) + jnp.dot(
+        dup.T, up_w, preferred_element_type=jnp.float32
     )
 
     @pl.when(step == 0)
@@ -162,6 +179,10 @@
     cap = count // 2
     owners = n_g // EXPERTS
     greet(n_g, n_s)
+    first, second, slot0, slot1 = slots(ids_ref)
+    width = n_g * cap
+    table[...] = pick(first, slot0, cap, owners, width) + pick(second, slot1, cap, owners, width)
+    met(n_g, n_s)
     mine = pl.ds(pl.multiple_of(g * cap, 16), cap)
 
     @pl.loop(1, n_s + 1)
@@ -182,10 +203,6 @@
 
         back[chunk, mine, :] = part_ref[mine, columns]
 
-    first, second, slot0, slot1 = slots(ids_ref)
-    width = n_g * cap
-    table[...] = pick(first, slot0, cap, owners, width) + pick(second, slot1, cap, owners, width)
-
     def arrived(chunk):
         whole = back.at[chunk, pl.ds(0, (n_g - 1) * cap), :]
         pltpu.make_async_copy(whole, whole, recv_a.at[chunk]).wait()
@@ -227,6 +244,7 @@
     cap = count // 2
     rows = n_g * cap
     hidden, width = gate_weight.shape[1:]
+    ids, probs = jnp.transpose(expert_ids), jnp.transpose(gate_probs)
     bf16 = jnp.bfloat16
     vmem = pl.BlockSpec(memory_space=pltpu.VMEM)
     dma = pltpu.SemaphoreType.DMA
@@ -245,7 +263,7 @@
             collective_id=0, has_side_effects=True, vmem_limit_bytes=BIG
         ),
         name="dispatch",
-    )(tokens, grad_out, expert_ids, gate_probs)
+    )(tokens, grad_out, ids, probs)
 
     block = block_of(hidden)
     steps = hidden // block
@@ -282,7 +300,7 @@
             collective_id=1, has_side_effects=True, vmem_limit_bytes=BIG
         ),
         name="give_back",
-    )(part, expert_ids)
+    )(part, ids)
     return grad_input, grad_down
 
 

time: 105 us -> 99.4 us (0.947)
  Pallas kernels: 100 us -> 97.1 us
  local copies, waits for them, and re-layouts: 4.15 us -> 1.42 us
    pallas_call x1, Pallas kernels: 53.5 us -> 50.2 us  [local(): pl.pallas_call(expert_kernel, grid=(steps,), out_shape=(jax.ShapeDtypeStr...]
    unnamed x3 -> x1, local copies, waits for them, and re-layouts: 4.15 us -> 1.42 us
where the time goes in v2:
time: 99.4 us; the launch traced here: 99.1 us
  Pallas kernels  97.1 us (98%)
  local copies, waits for them, and re-layouts  1.42 us (1%)
    pallas_call x1, Pallas kernels, local(): pl.pallas_call(expert_kernel, grid=(steps,), out_shape=(jax.ShapeDtypeStr...  50.2 us
    pallas_call x1, Pallas kernels, local(): pl.pallas_call(functools.partial(dispatch_kernel, n_g, n_s), out_shape=ja...  27.7 us
    pallas_call x1, Pallas kernels, local(): pl.pallas_call(functools.partial(return_kernel, n_g, n_s), out_shape=jax....  19.2 us

profile of v2, /device:TPU:0, one launch (start us, length us, event | category | flops | bytes accessed | tf_op | source)
XLA Modules:
  0.0 99.1 jit_solution(1518193141393343323)
XLA Ops:
  0.6 27.7 %dispatch.1.xg_ref = bf16[2,128,3072]{2,1,0:T(8,128)(2,1)} custom-call(bf16[32,768]{1,0:T(8,128)(2,1)} %tok_ref.1, bf16[32,768]{1,0:T(8,128)(2,1)} %grad_ref.1, s32[2,32]{1,0:T(2,128)} %bitcast.2, f32[2,32]{1,0:T(2,128)} %bitcast.4), custom_call_target="tpu_custom_call" | custom-call | tf_op jit(solution)/shard_map/dispatch/pallas_call | solution.py:251
  28.3 50.2 %experts.1 = (bf16[1,4608,3072]{2,1,0:T(8,128)(2,1)}, bf16[128,3072]{1,0:T(8,128)(2,1)}) custom-call(bf16[2,128,3072]{2,1,0:T(8,128)(2,1)} %dispatch.1.xg_ref, bf16[1,4608,3072]{2,1,0:T(8,128)(2,1)} %gate_ref.1, bf16[1,4608,3072]{2,1,0:T(8,128)(2,1)} %up_ref.1, bf16[1,4608,3072]{2,1,0:T(8,128)(2,1)} %down_ref.1), custom_call_target="tpu_custom_call" | custom-call | tf_op jit(solution)/shard_map/experts/pallas_call | solution.py:271
  78.5 19.2 %give_back.1 = bf16[32,768]{1,0:T(8,128)(2,1)} custom-call(bf16[128,3072]{1,0:T(8,128)(2,1)} %get-tuple-element.4.part_ref, s32[2,32]{1,0:T(2,128)} %bitcast.3), custom_call_target="tpu_custom_call" | custom-call | tf_op jit(solution)/shard_map/give_back/pallas_call | solution.py:287
  97.7 1.4 %copy.10 = bf16[32,768]{1,0:T(8,128)(2,1)} copy(bf16[32,768]{1,0:T(8,128)(2,1)} %give_back.1) | data formatting | bytes 98304
